TPU v7x, 32 devices: a whole 2x2x4 slice. The times are simulated.
32 devices in a mesh: tm: 8 (over z, x), fsdp: 4 (over y, core).
Axes of the slice: x: 2, y: 2, z: 4, core: 2. Of those that a mesh axis runs over, the one named last changes fastest.
Arguments:
- latents: bfloat16 [8192, 3072], P(('tm', 'fsdp')), may hold values from -6 to 6
- projected: bfloat16 [8192, 3, 512], P(('tm', 'fsdp')), may hold values from -20 to 20
- out_weight: bfloat16 [512, 3072], P(None, 'fsdp'), may hold values from -0.5 to 0.5
- gate_table: float32 [40, 3072], replicated, may hold values from 0.25 to 2
- timesteps: int32 [32], P('tm'), may hold values from 0 to 39
Outputs:
- updated: bfloat16 [8192, 3072], P(('tm', 'fsdp'))
All inputs are finite; a program needn't handle non-finite values.
Results may differ from a plain program's by a relative error of at most 0.0085.
Values may be sent and summed in bfloat16 or wider, within the bound.
A program may use at most 64 MiB of HBM per device.

v0:
```python
import jax
import jax.numpy as jnp
from jax import lax
from jax.sharding import PartitionSpec as P

FRAME_TOK = 256


def passed_along(value, axis, steps):
    count = lax.axis_size(axis)
    initial, last = (max(0, -steps), min(count, count - steps))
    return lax.ppermute(value, axis, [(source, source + steps) for source in range(initial, last)])


def attend(queries, extended, first_frame, frame_count):
    pair_rows = 2 * FRAME_TOK
    key_count = 5 * FRAME_TOK
    score_scale = queries.shape[1] ** (-0.5)
    row_frame = jnp.arange(pair_rows, dtype=jnp.int32) // FRAME_TOK
    col_frame = jnp.arange(key_count, dtype=jnp.int32) // FRAME_TOK

    def frame_pair(pair_index):
        offset = pair_index * pair_rows
        query_block = lax.dynamic_slice_in_dim(queries, offset, pair_rows, 0)
        window = lax.dynamic_slice_in_dim(extended, offset, key_count, 0)
        key_block = window[:, 0]
        value_block = window[:, 1]
        scores = (
            lax.dot_general(
                query_block, key_block, (((1,), (1,)), ((), ())), preferred_element_type=jnp.float32
            )
            * score_scale
        )
        distance = col_frame[None, :] - row_frame[:, None]
        existing = first_frame + 2 * pair_index + col_frame - 3 >= 0
        allowed = (distance >= 0) & (distance <= 3) & existing[None, :]
        scores = jnp.where(allowed, scores, -1e30)
        row_max = jnp.max(scores, axis=-1, keepdims=True)
        weights = jnp.exp(scores - row_max)
        row_sum = jnp.sum(weights, axis=-1, keepdims=True)
        probability = (weights / row_sum).astype(jnp.bfloat16)
        return jnp.dot(probability, value_block, preferred_element_type=jnp.float32).astype(
            jnp.bfloat16
        )

    blocks = lax.map(frame_pair, jnp.arange(frame_count // 2, dtype=jnp.int32))
    return blocks.reshape(frame_count * FRAME_TOK, queries.shape[1])


def body(latents, projected, out_weight, gate_table, timesteps):
    row_count = latents.shape[0]
    frame_count = timesteps.shape[0]
    group_tokens = frame_count * FRAME_TOK
    head_view = lax.all_to_all(projected, "fsdp", split_axis=2, concat_axis=0, tiled=True)
    queries = head_view[:, 0]
    key_values = head_view[:, 1:3]
    trailing = passed_along(key_values[group_tokens - 3 * FRAME_TOK :], "tm", 1)
    extended = jnp.concatenate([trailing, key_values], axis=0)
    first_frame = lax.axis_index("tm") * frame_count
    attended = attend(queries, extended, first_frame, frame_count)
    gathered_heads = lax.all_to_all(attended, "fsdp", split_axis=0, concat_axis=1, tiled=True)
    update = jnp.dot(
        gathered_heads,
        lax.all_gather(out_weight, "fsdp", axis=1, tiled=True),
        preferred_element_type=jnp.float32,
    )
    step_count = gate_table.shape[0]
    step_onehot = (timesteps[:, None] == jnp.arange(step_count, dtype=jnp.int32)[None, :]).astype(
        jnp.float32
    )
    frame_gates = jnp.dot(step_onehot, gate_table, precision=lax.Precision.HIGHEST)
    row_frame = (
        lax.axis_index("fsdp") * row_count + jnp.arange(row_count, dtype=jnp.int32)
    ) // FRAME_TOK
    row_onehot = (row_frame[:, None] == jnp.arange(frame_count, dtype=jnp.int32)[None, :]).astype(
        jnp.float32
    )
    row_gates = jnp.dot(row_onehot, frame_gates, precision=lax.Precision.HIGHEST)
    return (latents.astype(jnp.float32) + row_gates * update).astype(jnp.bfloat16)


def solution(mesh):
    in_specs = (
        P(("tm", "fsdp"), None),
        P(("tm", "fsdp"), None, None),
        P(None, "fsdp"),
        P(),
        P("tm"),
    )
    out_specs = P(("tm", "fsdp"), None)
    return jax.shard_map(body, mesh=mesh, in_specs=in_specs, out_specs=out_specs, check_vma=False)
```

profile of v0, /device:TPU:21, one launch (start us, length us, event | category | flops | bytes accessed | tf_op | source)
XLA Modules:
  0.0 81.5 jit_solution(7869486437224953958)
XLA Ops:
  6.5 0.0 copy-start
  6.5 0.0 all-gather.2.cloned.1.call-start
  6.5 0.7 all-gather.2.cloned.1.call-update
  7.3 1.6 %copy.10 = bf16[256,3,512]{0,1,2:T(4,128)(2,1)S(1)} copy(bf16[256,3,512]{2,0,1:T(8,128)(2,1)} %param.8) | data formatting | bytes 1572864 | tf_op args[1]
  8.9 21.4 %all_to_all.37 = bf16[256,3,512]{0,1,2:T(4,128)(2,1)S(1)} all-to-all(bf16[256,3,512]{0,1,2:T(4,128)(2,1)S(1)} %copy.10), channel_id=1, replica_groups=mesh['tm'=8,'fsdp'=4] {'fsdp'}, dimensions={2} | all-to-all | bytes 1572864 | tf_op jit(solution)/shard_map/all_to_all | solution.py:54
  30.3 0.7 copy.11
  31.0 3.1 %collective-permute-start = (bf16[768,2,128]{2,0,1:T(8,128)(2,1)S(1)}, bf16[768,2,128]{2,0,1:T(8,128)(2,1)S(1)}, u32[]{:S(2)}, u32[]{:S(2)}) collective-permute-start(bf16[768,2,128]{2,0,1:T(8,128)(2,1)S(1)} %slice.30), channel_id=1, source_target_pairs={{0,4},{4,8},{8,12},{12,16},{16,20},{20,24},{24,28},{1,5},{5,9},{9,... | collective-permute-start | bytes 1179656 | tf_op jit(solution)/shard_map/ppermute | solution.py:12
  34.2 9.3 %collective-permute-done = bf16[768,2,128]{2,0,1:T(8,128)(2,1)S(1)} collective-permute-done((bf16[768,2,128]{2,0,1:T(8,128)(2,1)S(1)}, bf16[768,2,128]{2,0,1:T(8,128)(2,1)S(1)}, u32[]{:S(2)}, u32[]{:S(2)}) %collective-permute-start) | collective-permute-done | bytes 393248 | tf_op jit(solution)/shard_map/ppermute | solution.py:12
  43.6 1.0 %pad_maximum_fusion = bf16[1792,2,128]{2,0,1:T(8,128)(2,1)} fusion(bf16[1024,2,128]{2,0,1:T(8,128)(2,1)S(1)} %slice.31, bf16[768,2,128]{2,0,1:T(8,128)(2,1)S(1)} %collective-permute-done), kind=kLoop, calls=%fused_computation.38 | loop fusion | flops 1835008 | bytes 1835008 | tf_op jit(solution)/shard_map/concatenate | solution.py:58
  44.6 0.0 copy-start.2
  44.6 13.4 %while.14 = (s32[]{:T(128)}, bf16[2,512,128]{2,1,0:T(8,128)(2,1)}, s32[2]{0:T(128)S(1)}, s32[]{:T(128)}, bf16[1024,128]{1,0:T(8,128)(2,1)S(1)}, /*index=5*/bf16[...) while((s32[]{:T(128)}, bf16[2,512,128]{2,1,0:T(8,128)(2,1)}, ...), condition=%wide.region_3.4_spmd.clone.clone, body=%wide.region_0.3_spmd.clone.clone.sunk | while | flops 344156928 | bytes 8813576 | solution.py:46
  44.6 0.6 dynamic_slice.32
  46.5 2.1 %fusion.35 = (f32[512]{0:T(512)S(1)}, f32[512,1280]{1,0:T(8,128)S(1)}) fusion(bf16[1792,2,128]{2,0,1:T(8,128)(2,1)} %get-tuple-element.231, s32[]{:T(128)S(6)} %select_n.71, bf16[1024,128]{1,0:T(8,128)(2,1)S(1)} %get-tuple-element.230, s32[]{:T(128)S(6)} %select_n.72, pred[1280]{0:T(1024)(128)(4,1)S(1)} %add_compare_fusion.2, ...), kind=kOutput, calls=%fused_computation.49.clone.1 | convolution fusion | flops 173014528 | bytes 3094536 | tf_op jit(solution)/shard_map/while/body/eval_jaxpr/dot_general | solution.py:29
  48.5 0.5 fusion.36
  49.0 2.2 %fusion.37 = bf16[2,512,128]{2,1,0:T(8,128)(2,1)} fusion(bf16[2,512,128]{2,1,0:T(8,128)(2,1)} %get-tuple-element.214, s32[]{:T(128)} %get-tuple-element.213, f32[512,1280]{1,0:T(8,128)S(1)} %get-tuple-element.198, f32[512]{0:T(512)S(1)} %fusion.36, f32[512]{0:T(512)S(1)} %get-tuple-element.199, bf16[1792,2,128]{2,0,1:T(8,128)(2,1)} %get-tuple-element.231, ...), kind=kOutput, calls=%fused_computation.14.clone.1 | convolution fusion | flops 169803776 | bytes 3084808 | tf_op jit(solution)/shard_map/while/body/eval_jaxpr/dot_general | solution.py:42
  51.3 0.6 dynamic_slice.32
  53.2 2.0 %fusion.35 = (f32[512]{0:T(512)S(1)}, f32[512,1280]{1,0:T(8,128)S(1)}) fusion(bf16[1792,2,128]{2,0,1:T(8,128)(2,1)} %get-tuple-element.231, s32[]{:T(128)S(6)} %select_n.71, bf16[1024,128]{1,0:T(8,128)(2,1)S(1)} %get-tuple-element.230, s32[]{:T(128)S(6)} %select_n.72, pred[1280]{0:T(1024)(128)(4,1)S(1)} %add_compare_fusion.2, ...), kind=kOutput, calls=%fused_computation.49.clone.1 | convolution fusion | flops 173014528 | bytes 3094536 | tf_op jit(solution)/shard_map/while/body/eval_jaxpr/dot_general | solution.py:29
  55.2 0.5 fusion.36
  55.7 2.2 %fusion.37 = bf16[2,512,128]{2,1,0:T(8,128)(2,1)} fusion(bf16[2,512,128]{2,1,0:T(8,128)(2,1)} %get-tuple-element.214, s32[]{:T(128)} %get-tuple-element.213, f32[512,1280]{1,0:T(8,128)S(1)} %get-tuple-element.198, f32[512]{0:T(512)S(1)} %fusion.36, f32[512]{0:T(512)S(1)} %get-tuple-element.199, bf16[1792,2,128]{2,0,1:T(8,128)(2,1)} %get-tuple-element.231, ...), kind=kOutput, calls=%fused_computation.14.clone.1 | convolution fusion | flops 169803776 | bytes 3084808 | tf_op jit(solution)/shard_map/while/body/eval_jaxpr/dot_general | solution.py:42
  58.0 6.4 %all-to-all-start.1 = ((bf16[4,256,128]{2,1,0:T(8,128)(2,1)}), bf16[4,256,128]{2,1,0:T(8,128)(2,1)S(1)}, u32[]{:S(2)}, u32[]{:S(2)}) async-start(bf16[4,256,128]{2,1,0:T(8,128)(2,1)} %bitcast.43), calls=%async_computation.1 | async-start | bytes 524288 | tf_op jit(solution)/shard_map/all_to_all | solution.py:61
  64.4 0.0 copy-done
  64.4 0.0 copy-done.2
  64.4 0.3 fusion.24
  64.7 3.8 %all-to-all-done.1 = bf16[4,256,128]{2,1,0:T(8,128)(2,1)S(1)} async-done(((bf16[4,256,128]{2,1,0:T(8,128)(2,1)}), bf16[4,256,128]{2,1,0:T(8,128)(2,1)S(1)}, u32[]{:S(2)}, u32[]{:S(2)}) %all-to-all-start.1) | async-done | bytes 262176 | tf_op jit(solution)/shard_map/all_to_all | solution.py:61
  68.5 0.1 copy.12
  68.7 0.0 all-gather.2.cloned.1.call-done
  68.7 0.0 copy-start.1
  68.7 3.0 %fusion.27 = f32[256,3072]{1,0:T(8,128)S(1)} fusion(bf16[256,512]{0,1:T(8,128)(2,1)S(1)} %bitcast.41, bf16[512,3072]{1,0:T(8,128)(2,1)} %all-gather.2.cloned.1.call-done), kind=kOutput, calls=%fused_computation.50 | convolution fusion | flops 805306368 | bytes 6553600 | tf_op jit(solution)/shard_map/dot_general | solution.py:62
  71.7 0.0 copy-done.1
  71.7 2.9 %fusion.22 = bf16[256,3072]{1,0:T(8,128)(2,1)} fusion(f32[256,3072]{1,0:T(8,128)S(1)} %fusion.27, f32[4,3072]{1,0:T(4,128)S(1)} %fusion.24, bf16[256,3072]{1,0:T(8,128)(2,1)S(1)} %copy-done.1, s32[256]{0:T(256)S(1)} %and_select_fusion), kind=kOutput, calls=%fused_computation.37 | convolution fusion | flops 40895488 | bytes 6341632 | tf_op jit(solution)/shard_map/dot_general | solution.py:78
  (12 shorter events, 0.1 us)
Async XLA Ops:
  6.5 57.8 %copy-start = (f32[40,3072]{1,0:T(8,128)S(1)}, f32[40,3072]{1,0:T(8,128)}, u32[]{:S(2)}) copy-start(f32[40,3072]{1,0:T(8,128)} %param.10) | copy-start | bytes 1474564
  6.5 62.1 %all-gather.2.cloned.1.call-start = ((), (), s32[]{:S(2)}) async-start(), calls=%async_computation.2 | async-start | bytes 3932160 | tf_op jit(solution)/shard_map/all_gather | solution.py:64
  31.0 12.6 %collective-permute-start = (bf16[768,2,128]{2,0,1:T(8,128)(2,1)S(1)}, bf16[768,2,128]{2,0,1:T(8,128)(2,1)S(1)}, u32[]{:S(2)}, u32[]{:S(2)}) collective-permute-start(bf16[768,2,128]{2,0,1:T(8,128)(2,1)S(1)} %slice.30), channel_id=1, source_target_pairs={{0,4},{4,8},{8,12},{12,16},{16,20},{20,24},{24,28},{1,5},{5,9},{9,... | collective-permute-start | bytes 1179656 | tf_op jit(solution)/shard_map/ppermute | solution.py:12
  44.6 19.8 %copy-start.2 = (s32[4]{0:T(128)S(1)}, s32[4]{0:T(128)}, u32[]{:S(2)}) copy-start(s32[4]{0:T(128)} %param.11) | copy-start | bytes 52
  58.0 10.5 %all-to-all-start.1 = ((bf16[4,256,128]{2,1,0:T(8,128)(2,1)}), bf16[4,256,128]{2,1,0:T(8,128)(2,1)S(1)}, u32[]{:S(2)}, u32[]{:S(2)}) async-start(bf16[4,256,128]{2,1,0:T(8,128)(2,1)} %bitcast.43), calls=%async_computation.1 | async-start | bytes 524288 | tf_op jit(solution)/shard_map/all_to_all | solution.py:61
  68.7 3.0 %copy-start.1 = (bf16[256,3072]{1,0:T(8,128)(2,1)S(1)}, bf16[256,3072]{1,0:T(8,128)(2,1)}, u32[]{:S(2)}) copy-start(bf16[256,3072]{1,0:T(8,128)(2,1)} %param.7) | copy-start | bytes 4718596
Sparse Core Ops, SparseCore 0:
  8.9 34.6 all-gather.1
where the time goes:
time: 83.1 us; the launch traced here: 81.5 us
  blocking collectives  21.4 us (26%)
  matrix products  14.8 us (18%)
  waiting for transfers between devices  13.9 us (17%)
  between operations  13.5 us (16%)
  starting transfers between devices  9.54 us (11%)
  local copies, waits for them, and re-layouts  3.74 us (5%)
  loops' own time  2.56 us (3%)
  other arithmetic  2.08 us (3%)
    all_to_all x1, blocking collectives, body(): lax.all_to_all(projected, 'fsdp', split_axis=2, concat_axis=0, tiled=True)  21.4 us
    ppermute x1, waiting for transfers between devices, passed_along(): lax.ppermute(value, axis, [(source, source + steps) for source in range(i...  9.32 us
    all_to_all x1, starting transfers between devices, body(): lax.all_to_all(attended, 'fsdp', split_axis=0, concat_axis=1, tiled=True)  6.4 us
    dot_general x2, matrix products, frame_pair(): jnp.dot(probability, value_block, preferred_element_type=jnp.float32)  4.48 us
    dot_general x2, matrix products, frame_pair(): lax.dot_general(query_block, key_block, (((1,), (1,)), ((), ())), preferr...  4.09 us
    all_to_all x1, waiting for transfers between devices, body(): lax.all_to_all(attended, 'fsdp', split_axis=0, concat_axis=1, tiled=True)  3.84 us
    ppermute x1, starting transfers between devices, passed_along(): lax.ppermute(value, axis, [(source, source + steps) for source in range(i...  3.14 us
    dot_general x1, matrix products, body(): jnp.dot(gathered_heads, lax.all_gather(out_weight, 'fsdp', axis=1, tiled=...  3.02 us
  transfers between devices with their start and end apart: 3, of which 2 were waited for; matrix products, arithmetic and copies ran while one was open for 18% of the time, Pallas kernels for 0%

commit v1 on v0

--- a/solution.py
+++ b/solution.py
@@ -1,6 +1,11 @@
+import functools
+import math
+
 import jax
 import jax.numpy as jnp
 from jax import lax
+from jax.experimental import pallas as pl
+from jax.experimental.pallas import tpu as pltpu
 from jax.sharding import PartitionSpec as P
 
 FRAME_TOK = 256
@@ -79,6 +84,331 @@
     return (latents.astype(jnp.float32) + row_gates * update).astype(jnp.bfloat16)
 
 
+HEAD = 128
+EARLY_WEIGHTS = (1, 2, 3)
+
+
+def by_member(member, values):
+    row, core = member // 2, member % 2
+    v0, v1, v2, v3 = values
+    return v0 + (v1 - v0) * core + (v2 - v0) * row + (v3 - v2 - v1 + v0) * core * row
+
+
+def frame_kernel(
+    groups,
+    steps_ref,
+    latents_hbm,
+    qkv_hbm,
+    weight_hbm,
+    gates_hbm,
+    out_hbm,
+    qkv,
+    kv,
+    weight,
+    latents,
+    gates,
+    gate_row,
+    out,
+    top,
+    total,
+    acc,
+    attended,
+    local_sem,
+    out_sem,
+    kv_send,
+    kv_pass,
+    kv_recv,
+    w_send,
+    w_pass,
+    w_recv,
+):
+    heads = kv.shape[1]
+    columns = weight.shape[2]
+    half = columns // 2
+    piece = half // 3
+    group, member = lax.axis_index("tm"), lax.axis_index("fsdp")
+    row, core = member // 2, member % 2
+    across = group + 1 - 2 * (group % 2)
+    sibling = member + 1 - 2 * core
+    opposite = member + 2 - 4 * row
+    far = 3 - member
+    has_next = jnp.logical_and(member >= 1, group < groups - 1)
+    has_previous = jnp.logical_and(member <= 2, group >= 1)
+
+    def remote(source, target, send_sem, recv_sem, to_group, to_member):
+        return pltpu.make_async_remote_copy(
+            src_ref=source,
+            dst_ref=target,
+            send_sem=send_sem,
+            recv_sem=recv_sem,
+            device_id=(to_group, to_member),
+            device_id_type=pl.DeviceIdType.MESH,
+        )
+
+    barrier = pltpu.get_barrier_semaphore()
+
+    def greet(to_group, to_member):
+        pl.semaphore_signal(
+            barrier, inc=1, device_id=(to_group, to_member), device_id_type=pl.DeviceIdType.MESH
+        )
+
+    greet(group, sibling)
+    greet(group, opposite)
+    greet(across, member)
+
+    @pl.when(has_next)
+    def _():
+        greet(group + 1, member - 1)
+
+    @pl.when(has_previous)
+    def _():
+        greet(group - 1, member + 1)
+
+    load_qkv = pltpu.make_async_copy(qkv_hbm, qkv, local_sem.at[0])
+    load_weight = pltpu.make_async_copy(weight_hbm, weight.at[member], local_sem.at[1])
+    load_latents = pltpu.make_async_copy(latents_hbm, latents, local_sem.at[2])
+    load_gates = pltpu.make_async_copy(gates_hbm, gates, local_sem.at[3])
+    load_qkv.start()
+    load_weight.start()
+    load_gates.start()
+    load_latents.start()
+
+    pl.semaphore_wait(barrier, 3 + has_next.astype(jnp.int32) + has_previous.astype(jnp.int32))
+
+    sent = []
+
+    def begin(condition, copy):
+        sent.append((condition, copy))
+        if condition is None:
+            copy.start()
+        else:
+            pl.when(condition)(copy.start)
+
+    for h in range(heads):
+        own = qkv_hbm.at[pl.ds(1, 2), :, pl.ds(h * HEAD, HEAD)]
+        begin(
+            row == 0,
+            remote(own, kv.at[1, h], kv_send.at[0, h], kv_recv.at[1, h], group, opposite),
+        )
+        begin(
+            has_next,
+            remote(own, kv.at[2, h], kv_send.at[1, h], kv_recv.at[2, h], group + 1, member - 1),
+        )
+        begin(
+            core == 0,
+            remote(own, kv.at[0, h], kv_send.at[2, h], kv_recv.at[0, h], group, sibling),
+        )
+
+    first = pl.multiple_of(half * (group % 2), 128)
+    second = pl.multiple_of(half - half * (group % 2), 128)
+
+    def cut(start, index):
+        return pl.ds(pl.multiple_of(start + index * piece, 128), piece)
+
+    for i in range(3):
+        begin(
+            None,
+            remote(
+                weight_hbm.at[:, cut(first, i)],
+                weight.at[member, :, cut(first, i)],
+                w_send.at[i],
+                w_recv.at[i],
+                group,
+                opposite,
+            ),
+        )
+    begin(
+        None,
+        remote(weight_hbm, weight.at[member], w_send.at[3], w_recv.at[6], group, sibling),
+    )
+
+    def arrived(target, sem):
+        remote(target, target, w_send.at[0], sem, group, sibling).wait_recv()
+
+    def take_piece(i):
+        start = first if i < 3 else second
+        block = weight.at[opposite, :, cut(start, i % 3)]
+        arrived(block, w_recv.at[i])
+        if i < 3:
+            begin(
+                None,
+                remote(block, block, w_pass.at[i], w_recv.at[3 + i], across, member),
+            )
+        begin(
+            None,
+            remote(block, block, w_pass.at[3 + i], w_recv.at[7 + i], group, sibling),
+        )
+
+    scale = (HEAD ** -0.5) * math.log2(math.e)
+
+    def own_head(index, h):
+        return qkv[index, :, h * HEAD : (h + 1) * HEAD]
+
+    def scores_of(h, keys):
+        return (
+            lax.dot_general(
+                own_head(0, h), keys, (((1,), (1,)), ((), ())), preferred_element_type=jnp.float32
+            )
+            * scale
+        )
+
+    def start_head(h):
+        scores = scores_of(h, own_head(1, h))
+        row_top = jnp.max(scores, axis=-1, keepdims=True)
+        weights = jnp.exp2(scores - row_top)
+        top[h] = row_top
+        total[h] = jnp.sum(weights, axis=-1, keepdims=True)
+        acc[h] = jnp.dot(
+            weights.astype(jnp.bfloat16), own_head(2, h), preferred_element_type=jnp.float32
+        )
+
+    def add_frame(h, slot):
+        scores = scores_of(h, kv[slot, h, 0])
+        old_top = top[h]
+        row_top = jnp.maximum(old_top, jnp.max(scores, axis=-1, keepdims=True))
+        weights = jnp.exp2(scores - row_top)
+        shrink = jnp.exp2(old_top - row_top)
+        top[h] = row_top
+        total[h] = total[h] * shrink + jnp.sum(weights, axis=-1, keepdims=True)
+        acc[h] = acc[h] * shrink + jnp.dot(
+            weights.astype(jnp.bfloat16), kv[slot, h, 1], preferred_element_type=jnp.float32
+        )
+
+    order = ((3, 1, 2, 1), (1, 3, 3, 2), (2, 2, 1, 3))
+
+    def take_frame(j, h):
+        back = by_member(member, order[j])
+        slot = back - 1
+        exists = jnp.logical_or(group >= 1, member >= back)
+        block = kv.at[slot, h]
+
+        pl.when(exists)(lambda: arrived(block, kv_recv.at[slot, h]))
+        if j == 0:
+            begin(
+                jnp.logical_and(exists, member == 2),
+                remote(block, kv.at[2, h], kv_pass.at[0, h], kv_recv.at[2, h], group, sibling),
+            )
+        if j == 1:
+            to = by_member(member, (1, 0, 0, 2))
+            into = by_member(member, (1, 1, 0, 0))
+            begin(
+                exists,
+                remote(block, kv.at[into, h], kv_pass.at[1, h], kv_recv.at[into, h], group, to),
+            )
+        pl.when(exists)(lambda: add_frame(h, slot))
+
+    load_qkv.wait()
+    for h in range(heads):
+        start_head(h)
+    load_gates.wait()
+    step_index = lax.broadcasted_iota(jnp.int32, gates.shape, 0)
+    gate_row[...] = jnp.sum(
+        jnp.where(step_index == steps_ref[member], gates[...], 0.0), axis=0, keepdims=True
+    )
+
+    def finish_head(h):
+        attended[:, h * HEAD : (h + 1) * HEAD] = (acc[h] / total[h]).astype(jnp.bfloat16)
+
+    for h in range(heads):
+        take_frame(0, h)
+        take_frame(1, h)
+        if h >= 1:
+            take_frame(2, h - 1)
+            finish_head(h - 1)
+        if h in EARLY_WEIGHTS:
+            take_piece(EARLY_WEIGHTS.index(h))
+    take_frame(2, heads - 1)
+    finish_head(heads - 1)
+
+    writes = []
+
+    def project(owner, start, width):
+        place = pl.ds(pl.multiple_of(owner * columns + start, 128), width)
+        branch = jnp.dot(
+            attended[...],
+            weight[owner, :, pl.ds(start, width)],
+            preferred_element_type=jnp.float32,
+        )
+        out[:, place] = (
+            latents[:, place].astype(jnp.float32) + gate_row[:, place] * branch
+        ).astype(jnp.bfloat16)
+        write = pltpu.make_async_copy(
+            out.at[:, place], out_hbm.at[:, place], out_sem.at[len(writes)]
+        )
+        write.start()
+        writes.append(write)
+
+    load_weight.wait()
+    load_latents.wait()
+    project(member, 0, half)
+    project(member, half, half)
+    take_piece(3)
+    arrived(weight.at[sibling], w_recv.at[6])
+    project(sibling, 0, half)
+    project(sibling, half, half)
+    take_piece(4)
+    project(opposite, first, half)
+    take_piece(5)
+    project(opposite, second, half)
+    for i in range(3):
+        arrived(weight.at[far, :, cut(first, i)], w_recv.at[7 + i])
+    project(far, first, half)
+    for i in range(3):
+        arrived(weight.at[far, :, cut(second, i)], w_recv.at[10 + i])
+    project(far, second, half)
+
+    for condition, copy in sent:
+        if condition is None:
+            copy.wait_send()
+        else:
+            pl.when(condition)(copy.wait_send)
+    for write in writes:
+        write.wait()
+
+
+def frame_body(latents, projected, out_weight, gate_table, timesteps, groups):
+    rows, width = latents.shape
+    inner, columns = out_weight.shape
+    heads = inner // HEAD
+    qkv = projected.transpose(1, 0, 2)
+    anywhere = pl.BlockSpec(memory_space=pl.ANY)
+    return pl.pallas_call(
+        functools.partial(frame_kernel, groups),
+        out_shape=jax.ShapeDtypeStruct((rows, width), jnp.bfloat16),
+        in_specs=[pl.BlockSpec(memory_space=pltpu.SMEM)] + [anywhere] * 4,
+        out_specs=anywhere,
+        scratch_shapes=[
+            pltpu.VMEM((3, rows, inner), jnp.bfloat16),
+            pltpu.VMEM((3, heads, 2, rows, HEAD), jnp.bfloat16),
+            pltpu.VMEM((4, inner, columns), jnp.bfloat16),
+            pltpu.VMEM((rows, width), jnp.bfloat16),
+            pltpu.VMEM(gate_table.shape, jnp.float32),
+            pltpu.VMEM((1, width), jnp.float32),
+            pltpu.VMEM((rows, width), jnp.bfloat16),
+            pltpu.VMEM((heads, rows, 1), jnp.float32),
+            pltpu.VMEM((heads, rows, 1), jnp.float32),
+            pltpu.VMEM((heads, rows, HEAD), jnp.float32),
+            pltpu.VMEM((rows, inner), jnp.bfloat16),
+            pltpu.SemaphoreType.DMA((4,)),
+            pltpu.SemaphoreType.DMA((8,)),
+            pltpu.SemaphoreType.DMA((3, heads)),
+            pltpu.SemaphoreType.DMA((2, heads)),
+            pltpu.SemaphoreType.DMA((3, heads)),
+            pltpu.SemaphoreType.DMA((4,)),
+            pltpu.SemaphoreType.DMA((9,)),
+            pltpu.SemaphoreType.DMA((13,)),
+        ],
+        compiler_params=pltpu.CompilerParams(
+            collective_id=0, has_side_effects=True, vmem_limit_bytes=60 * 1024 * 1024
+        ),
+        cost_estimate=pl.CostEstimate(
+            flops=2 * rows * inner * (8 * rows + width),
+            bytes_accessed=4 * rows * width + 2 * inner * width,
+            transcendentals=4 * heads * rows * rows,
+        ),
+    )(timesteps, latents, qkv, out_weight, gate_table)
+
+
 def solution(mesh):
     in_specs = (
         P(("tm", "fsdp"), None),
@@ -88,4 +418,12 @@
         P("tm"),
     )
     out_specs = P(("tm", "fsdp"), None)
-    return jax.shard_map(body, mesh=mesh, in_specs=in_specs, out_specs=out_specs, check_vma=False)
+    groups, members = mesh.shape["tm"], mesh.shape["fsdp"]
+
+    def local(latents, projected, out_weight, gate_table, timesteps):
+        one_frame_each = latents.shape[0] == FRAME_TOK and timesteps.shape[0] == members
+        if one_frame_each and members == 4 and groups % 2 == 0:
+            return frame_body(latents, projected, out_weight, gate_table, timesteps, groups)
+        return body(latents, projected, out_weight, gate_table, timesteps)
+
+    return jax.shard_map(local, mesh=mesh, in_specs=in_specs, out_specs=out_specs, check_vma=False)

time: 83.1 us -> 40 us (0.48)
  the two profiles are of different devices: /device:TPU:21 before, /device:TPU:1 now
where the time goes in v1:
time: 40 us; the launch traced here: 39.8 us
  Pallas kernels  37.2 us (93%)
  local copies, waits for them, and re-layouts  2.65 us (7%)
    pallas_call x1, Pallas kernels, frame_body(): pl.pallas_call(functools.partial(frame_kernel, groups), out_shape=jax.Sha...  37.2 us
    unnamed x1, local copies, waits for them, and re-layouts  2.65 us

profile of v1, /device:TPU:1, one launch (start us, length us, event | category | flops | bytes accessed | tf_op | source)
XLA Modules:
  0.0 39.8 jit_solution(15660455561878019485)
XLA Ops:
  0.0 37.2 %shard_map.55 = bf16[256,3072]{1,0:T(8,128)(2,1)} custom-call(s32[4]{0:T(128)} %steps_ref.1, bf16[256,3072]{1,0:T(8,128)(2,1)} %latents_hbm.1, bf16[3,256,512]{2,1,0:T(8,128)(2,1)} %bitcast.1, bf16[512,768]{1,0:T(8,128)(2,1)} %weight_hbm.1, f32[40,3072]{1,0:T(8,128)} %gates_hbm.1), custom_call_target="tpu_custom_call" | custom-call | flops 1342177280 | bytes 6291456 | tf_op jit(solution)/shard_map/pallas_call | solution.py:375
  37.2 2.7 %copy.7 = bf16[256,3072]{1,0:T(8,128)(2,1)} copy(bf16[256,3072]{1,0:T(8,128)(2,1)} %shard_map.55) | data formatting | bytes 3145728

commit v2 on v1

--- a/solution.py
+++ b/solution.py
@@ -85,7 +85,6 @@
 
 
 HEAD = 128
-EARLY_WEIGHTS = (1, 2, 3)
 
 
 def by_member(member, values):
@@ -101,20 +100,18 @@
     qkv_hbm,
     weight_hbm,
     gates_hbm,
-    out_hbm,
+    out,
     qkv,
     kv,
     weight,
     latents,
     gates,
     gate_row,
-    out,
     top,
     total,
     acc,
     attended,
     local_sem,
-    out_sem,
     kv_send,
     kv_pass,
     kv_recv,
@@ -205,7 +202,7 @@
     def cut(start, index):
         return pl.ds(pl.multiple_of(start + index * piece, 128), piece)
 
-    for i in range(3):
+    def send_piece(i):
         begin(
             None,
             remote(
@@ -217,10 +214,12 @@
                 opposite,
             ),
         )
-    begin(
-        None,
-        remote(weight_hbm, weight.at[member], w_send.at[3], w_recv.at[6], group, sibling),
-    )
+
+    def send_sibling():
+        begin(
+            None,
+            remote(weight_hbm, weight.at[member], w_send.at[3], w_recv.at[6], group, sibling),
+        )
 
     def arrived(target, sem):
         remote(target, target, w_send.at[0], sem, group, sibling).wait_recv()
@@ -276,12 +275,13 @@
 
     order = ((3, 1, 2, 1), (1, 3, 3, 2), (2, 2, 1, 3))
 
-    def take_frame(j, h):
+    def place_of(j):
         back = by_member(member, order[j])
-        slot = back - 1
-        exists = jnp.logical_or(group >= 1, member >= back)
+        return back - 1, jnp.logical_or(group >= 1, member >= back)
+
+    def receive(j, h):
+        slot, exists = place_of(j)
         block = kv.at[slot, h]
-
         pl.when(exists)(lambda: arrived(block, kv_recv.at[slot, h]))
         if j == 0:
             begin(
@@ -295,6 +295,9 @@
                 exists,
                 remote(block, kv.at[into, h], kv_pass.at[1, h], kv_recv.at[into, h], group, to),
             )
+
+    def attend_frame(j, h):
+        slot, exists = place_of(j)
         pl.when(exists)(lambda: add_frame(h, slot))
 
     load_qkv.wait()
@@ -310,17 +313,21 @@
         attended[:, h * HEAD : (h + 1) * HEAD] = (acc[h] / total[h]).astype(jnp.bfloat16)
 
     for h in range(heads):
-        take_frame(0, h)
-        take_frame(1, h)
+        receive(0, h)
+        receive(1, h)
+        if h == 1:
+            send_sibling()
         if h >= 1:
-            take_frame(2, h - 1)
+            send_piece(h - 1)
+            receive(2, h - 1)
+        attend_frame(0, h)
+        attend_frame(1, h)
+        if h >= 1:
+            attend_frame(2, h - 1)
             finish_head(h - 1)
-        if h in EARLY_WEIGHTS:
-            take_piece(EARLY_WEIGHTS.index(h))
-    take_frame(2, heads - 1)
+    receive(2, heads - 1)
+    attend_frame(2, heads - 1)
     finish_head(heads - 1)
-
-    writes = []
 
     def project(owner, start, width):
         place = pl.ds(pl.multiple_of(owner * columns + start, 128), width)
@@ -332,27 +339,25 @@
         out[:, place] = (
             latents[:, place].astype(jnp.float32) + gate_row[:, place] * branch
         ).astype(jnp.bfloat16)
-        write = pltpu.make_async_copy(
-            out.at[:, place], out_hbm.at[:, place], out_sem.at[len(writes)]
-        )
-        write.start()
-        writes.append(write)
 
     load_weight.wait()
     load_latents.wait()
+    take_piece(0)
     project(member, 0, half)
+    take_piece(1)
     project(member, half, half)
-    take_piece(3)
+    take_piece(2)
     arrived(weight.at[sibling], w_recv.at[6])
     project(sibling, 0, half)
     project(sibling, half, half)
+    take_piece(3)
+    project(opposite, first, half)
     take_piece(4)
-    project(opposite, first, half)
-    take_piece(5)
-    project(opposite, second, half)
     for i in range(3):
         arrived(weight.at[far, :, cut(first, i)], w_recv.at[7 + i])
     project(far, first, half)
+    take_piece(5)
+    project(opposite, second, half)
     for i in range(3):
         arrived(weight.at[far, :, cut(second, i)], w_recv.at[10 + i])
     project(far, second, half)
@@ -362,8 +367,6 @@
             copy.wait_send()
         else:
             pl.when(condition)(copy.wait_send)
-    for write in writes:
-        write.wait()
 
 
 def frame_body(latents, projected, out_weight, gate_table, timesteps, groups):
@@ -371,12 +374,12 @@
     inner, columns = out_weight.shape
     heads = inner // HEAD
     qkv = projected.transpose(1, 0, 2)
-    anywhere = pl.BlockSpec(memory_space=pl.ANY)
+    in_hbm = pl.BlockSpec(memory_space=pltpu.HBM)
     return pl.pallas_call(
         functools.partial(frame_kernel, groups),
-        out_shape=jax.ShapeDtypeStruct((rows, width), jnp.bfloat16),
-        in_specs=[pl.BlockSpec(memory_space=pltpu.SMEM)] + [anywhere] * 4,
-        out_specs=anywhere,
+        out_shape=pltpu.VMEM((rows, width), jnp.bfloat16),
+        in_specs=[pl.BlockSpec(memory_space=pltpu.SMEM)] + [in_hbm] * 4,
+        out_specs=pl.BlockSpec(memory_space=pltpu.VMEM),
         scratch_shapes=[
             pltpu.VMEM((3, rows, inner), jnp.bfloat16),
             pltpu.VMEM((3, heads, 2, rows, HEAD), jnp.bfloat16),
@@ -384,13 +387,11 @@
             pltpu.VMEM((rows, width), jnp.bfloat16),
             pltpu.VMEM(gate_table.shape, jnp.float32),
             pltpu.VMEM((1, width), jnp.float32),
-            pltpu.VMEM((rows, width), jnp.bfloat16),
             pltpu.VMEM((heads, rows, 1), jnp.float32),
             pltpu.VMEM((heads, rows, 1), jnp.float32),
             pltpu.VMEM((heads, rows, HEAD), jnp.float32),
             pltpu.VMEM((rows, inner), jnp.bfloat16),
             pltpu.SemaphoreType.DMA((4,)),
-            pltpu.SemaphoreType.DMA((8,)),
             pltpu.SemaphoreType.DMA((3, heads)),
             pltpu.SemaphoreType.DMA((2, heads)),
             pltpu.SemaphoreType.DMA((3, heads)),
@@ -399,7 +400,7 @@
             pltpu.SemaphoreType.DMA((13,)),
         ],
         compiler_params=pltpu.CompilerParams(
-            collective_id=0, has_side_effects=True, vmem_limit_bytes=60 * 1024 * 1024
+            collective_id=0, has_side_effects=True, vmem_limit_bytes=56 * 1024 * 1024
         ),
         cost_estimate=pl.CostEstimate(
             flops=2 * rows * inner * (8 * rows + width),

time: 40 us -> 43.4 us (1.085)
  Pallas kernels: 37.2 us -> 42.1 us
  local copies, waits for them, and re-layouts: 2.65 us -> 1.15 us
    pallas_call x1, Pallas kernels: 37.2 us -> 42.1 us  [frame_body(): pl.pallas_call(functools.partial(frame_kernel, groups), out_shape=pltpu.V...]
    unnamed x1, local copies, waits for them, and re-layouts: 2.65 us -> 1.15 us
where the time goes in v2:
time: 43.4 us; the launch traced here: 43.3 us
  Pallas kernels  42.1 us (97%)
  local copies, waits for them, and re-layouts  1.15 us (3%)
    pallas_call x1, Pallas kernels, frame_body(): pl.pallas_call(functools.partial(frame_kernel, groups), out_shape=pltpu.V...  42.1 us
    unnamed x1, local copies, waits for them, and re-layouts  1.15 us

profile of v2, /device:TPU:1, one launch (start us, length us, event | category | flops | bytes accessed | tf_op | source)
XLA Modules:
  0.0 43.3 jit_solution(10875193653253296356)
XLA Ops:
  0.0 42.1 %shard_map.55 = bf16[256,3072]{1,0:T(8,128)(2,1)S(1)} custom-call(s32[4]{0:T(128)} %steps_ref.1, bf16[256,3072]{1,0:T(8,128)(2,1)} %latents_hbm.1, bf16[3,256,512]{2,1,0:T(8,128)(2,1)} %bitcast.1, bf16[512,768]{1,0:T(8,128)(2,1)} %weight_hbm.1, f32[40,3072]{1,0:T(8,128)} %gates_hbm.1), custom_call_target="tpu_custom_call" | custom-call | flops 1342177280 | bytes 6291456 | tf_op jit(solution)/shard_map/pallas_call | solution.py:378
  42.1 1.1 %copy.7 = bf16[256,3072]{1,0:T(8,128)(2,1)} copy(bf16[256,3072]{1,0:T(8,128)(2,1)S(1)} %shard_map.55) | data formatting | bytes 3145728

commit v3 on v2

--- a/solution.py
+++ b/solution.py
@@ -181,19 +181,25 @@
         else:
             pl.when(condition)(copy.start)
 
-    for h in range(heads):
-        own = qkv_hbm.at[pl.ds(1, 2), :, pl.ds(h * HEAD, HEAD)]
+    def own_block(h):
+        return qkv_hbm.at[pl.ds(1, 2), :, pl.ds(h * HEAD, HEAD)]
+
+    def send_opposite(h):
         begin(
             row == 0,
-            remote(own, kv.at[1, h], kv_send.at[0, h], kv_recv.at[1, h], group, opposite),
-        )
+            remote(own_block(h), kv.at[1, h], kv_send.at[0, h], kv_recv.at[1, h], group, opposite),
+        )
+
+    def send_near(h):
         begin(
             has_next,
-            remote(own, kv.at[2, h], kv_send.at[1, h], kv_recv.at[2, h], group + 1, member - 1),
+            remote(
+                own_block(h), kv.at[2, h], kv_send.at[1, h], kv_recv.at[2, h], group + 1, member - 1
+            ),
         )
         begin(
             core == 0,
-            remote(own, kv.at[0, h], kv_send.at[2, h], kv_recv.at[0, h], group, sibling),
+            remote(own_block(h), kv.at[0, h], kv_send.at[2, h], kv_recv.at[0, h], group, sibling),
         )
 
     first = pl.multiple_of(half * (group % 2), 128)
@@ -246,34 +252,38 @@
     def scores_of(h, keys):
         return (
             lax.dot_general(
-                own_head(0, h), keys, (((1,), (1,)), ((), ())), preferred_element_type=jnp.float32
+                keys, own_head(0, h), (((1,), (1,)), ((), ())), preferred_element_type=jnp.float32
             )
             * scale
         )
 
+    def mix(values, weights):
+        return lax.dot_general(
+            values,
+            weights.astype(jnp.bfloat16),
+            (((0,), (0,)), ((), ())),
+            preferred_element_type=jnp.float32,
+        )
+
     def start_head(h):
         scores = scores_of(h, own_head(1, h))
-        row_top = jnp.max(scores, axis=-1, keepdims=True)
+        row_top = jnp.max(scores, axis=0, keepdims=True)
         weights = jnp.exp2(scores - row_top)
         top[h] = row_top
-        total[h] = jnp.sum(weights, axis=-1, keepdims=True)
-        acc[h] = jnp.dot(
-            weights.astype(jnp.bfloat16), own_head(2, h), preferred_element_type=jnp.float32
-        )
+        total[h] = jnp.sum(weights, axis=0, keepdims=True)
+        acc[h] = mix(own_head(2, h), weights)
 
     def add_frame(h, slot):
         scores = scores_of(h, kv[slot, h, 0])
         old_top = top[h]
-        row_top = jnp.maximum(old_top, jnp.max(scores, axis=-1, keepdims=True))
+        row_top = jnp.maximum(old_top, jnp.max(scores, axis=0, keepdims=True))
         weights = jnp.exp2(scores - row_top)
         shrink = jnp.exp2(old_top - row_top)
         top[h] = row_top
-        total[h] = total[h] * shrink + jnp.sum(weights, axis=-1, keepdims=True)
-        acc[h] = acc[h] * shrink + jnp.dot(
-            weights.astype(jnp.bfloat16), kv[slot, h, 1], preferred_element_type=jnp.float32
-        )
-
-    order = ((3, 1, 2, 1), (1, 3, 3, 2), (2, 2, 1, 3))
+        total[h] = total[h] * shrink + jnp.sum(weights, axis=0, keepdims=True)
+        acc[h] = acc[h] * shrink + mix(kv[slot, h, 1], weights)
+
+    order = ((3, 1, 3, 1), (1, 3, 2, 2), (2, 2, 1, 3))
 
     def place_of(j):
         back = by_member(member, order[j])
@@ -286,41 +296,61 @@
         if j == 0:
             begin(
                 jnp.logical_and(exists, member == 2),
-                remote(block, kv.at[2, h], kv_pass.at[0, h], kv_recv.at[2, h], group, sibling),
+                remote(block, kv.at[0, h], kv_pass.at[0, h], kv_recv.at[0, h], group, opposite),
             )
         if j == 1:
-            to = by_member(member, (1, 0, 0, 2))
-            into = by_member(member, (1, 1, 0, 0))
+            into = by_member(member, (1, 1, 2, 0))
             begin(
                 exists,
-                remote(block, kv.at[into, h], kv_pass.at[1, h], kv_recv.at[into, h], group, to),
+                remote(
+                    block, kv.at[into, h], kv_pass.at[1, h], kv_recv.at[into, h], group, sibling
+                ),
             )
 
     def attend_frame(j, h):
         slot, exists = place_of(j)
         pl.when(exists)(lambda: add_frame(h, slot))
 
+    def finish_head(h):
+        attended[:, h * HEAD : (h + 1) * HEAD] = jnp.transpose(acc[h] / total[h]).astype(jnp.bfloat16)
+
+    for i in range(3):
+        send_piece(i)
+        send_near(i)
+    for h in range(3, heads):
+        send_near(h)
+    send_opposite(0)
+    send_sibling()
+
     load_qkv.wait()
-    for h in range(heads):
+    start_head(0)
+    start_head(1)
+    receive(0, 0)
+    receive(0, 1)
+    take_piece(0)
+    send_opposite(1)
+    for h in range(2, heads):
         start_head(h)
+        receive(0, h)
+    attend_frame(0, 0)
+    attend_frame(0, 1)
+    take_piece(1)
+    send_opposite(2)
+    for h in range(2, heads):
+        attend_frame(0, h)
     load_gates.wait()
     step_index = lax.broadcasted_iota(jnp.int32, gates.shape, 0)
     gate_row[...] = jnp.sum(
         jnp.where(step_index == steps_ref[member], gates[...], 0.0), axis=0, keepdims=True
     )
-
-    def finish_head(h):
-        attended[:, h * HEAD : (h + 1) * HEAD] = (acc[h] / total[h]).astype(jnp.bfloat16)
-
+    take_piece(2)
+    for h in range(3, heads):
+        send_opposite(h)
     for h in range(heads):
-        receive(0, h)
         receive(1, h)
-        if h == 1:
-            send_sibling()
         if h >= 1:
-            send_piece(h - 1)
             receive(2, h - 1)
-        attend_frame(0, h)
+            take_piece(2 + min(h, 3))
         attend_frame(1, h)
         if h >= 1:
             attend_frame(2, h - 1)
@@ -342,25 +372,17 @@
 
     load_weight.wait()
     load_latents.wait()
-    take_piece(0)
     project(member, 0, half)
-    take_piece(1)
     project(member, half, half)
-    take_piece(2)
     arrived(weight.at[sibling], w_recv.at[6])
     project(sibling, 0, half)
     project(sibling, half, half)
-    take_piece(3)
     project(opposite, first, half)
-    take_piece(4)
-    for i in range(3):
-        arrived(weight.at[far, :, cut(first, i)], w_recv.at[7 + i])
-    project(far, first, half)
-    take_piece(5)
     project(opposite, second, half)
-    for i in range(3):
-        arrived(weight.at[far, :, cut(second, i)], w_recv.at[10 + i])
-    project(far, second, half)
+    for i in range(6):
+        arrived(weight.at[far, :, cut(first if i < 3 else second, i % 3)], w_recv.at[7 + i])
+        if i % 3 == 2:
+            project(far, first if i < 3 else second, half)
 
     for condition, copy in sent:
         if condition is None:
@@ -387,9 +409,9 @@
             pltpu.VMEM((rows, width), jnp.bfloat16),
             pltpu.VMEM(gate_table.shape, jnp.float32),
             pltpu.VMEM((1, width), jnp.float32),
-            pltpu.VMEM((heads, rows, 1), jnp.float32),
-            pltpu.VMEM((heads, rows, 1), jnp.float32),
-            pltpu.VMEM((heads, rows, HEAD), jnp.float32),
+            pltpu.VMEM((heads, 1, rows), jnp.float32),
+            pltpu.VMEM((heads, 1, rows), jnp.float32),
+            pltpu.VMEM((heads, HEAD, rows), jnp.float32),
             pltpu.VMEM((rows, inner), jnp.bfloat16),
             pltpu.SemaphoreType.DMA((4,)),
             pltpu.SemaphoreType.DMA((3, heads)),

time: 43.4 us -> 30.3 us (0.70)
  the two profiles are of different devices: /device:TPU:1 before, /device:TPU:3 now
where the time goes in v3:
time: 30.3 us; the launch traced here: 30.2 us
  Pallas kernels  29 us (96%)
  local copies, waits for them, and re-layouts  1.15 us (4%)
    pallas_call x1, Pallas kernels, frame_body(): pl.pallas_call(functools.partial(frame_kernel, groups), out_shape=pltpu.V...  29 us
    unnamed x1, local copies, waits for them, and re-layouts  1.15 us

profile of v3, /device:TPU:3, one launch (start us, length us, event | category | flops | bytes accessed | tf_op | source)
XLA Modules:
  0.0 30.2 jit_solution(10054937546088861217)
XLA Ops:
  0.0 29.0 %shard_map.55 = bf16[256,3072]{1,0:T(8,128)(2,1)S(1)} custom-call(s32[4]{0:T(128)} %steps_ref.1, bf16[256,3072]{1,0:T(8,128)(2,1)} %latents_hbm.1, bf16[3,256,512]{2,1,0:T(8,128)(2,1)} %bitcast.1, bf16[512,768]{1,0:T(8,128)(2,1)} %weight_hbm.1, f32[40,3072]{1,0:T(8,128)} %gates_hbm.1), custom_call_target="tpu_custom_call" | custom-call | flops 1342177280 | bytes 6291456 | tf_op jit(solution)/shard_map/pallas_call | solution.py:400
  29.0 1.1 %copy.7 = bf16[256,3072]{1,0:T(8,128)(2,1)} copy(bf16[256,3072]{1,0:T(8,128)(2,1)S(1)} %shard_map.55) | data formatting | bytes 3145728

commit v4 on v3

--- a/solution.py
+++ b/solution.py
@@ -122,10 +122,11 @@
     heads = kv.shape[1]
     columns = weight.shape[2]
     half = columns // 2
-    piece = half // 3
+    piece = weight.shape[1] // 8
     group, member = lax.axis_index("tm"), lax.axis_index("fsdp")
     row, core = member // 2, member % 2
-    across = group + 1 - 2 * (group % 2)
+    beside = group + 1 - 2 * (group % 2)
+    along = group + 2 - 4 * ((group // 2) % 2)
     sibling = member + 1 - 2 * core
     opposite = member + 2 - 4 * row
     far = 3 - member
@@ -151,7 +152,8 @@
 
     greet(group, sibling)
     greet(group, opposite)
-    greet(across, member)
+    greet(beside, member)
+    greet(along, member)
 
     @pl.when(has_next)
     def _():
@@ -170,7 +172,7 @@
     load_gates.start()
     load_latents.start()
 
-    pl.semaphore_wait(barrier, 3 + has_next.astype(jnp.int32) + has_previous.astype(jnp.int32))
+    pl.semaphore_wait(barrier, 4 + has_next.astype(jnp.int32) + has_previous.astype(jnp.int32))
 
     sent = []
 
@@ -202,20 +204,25 @@
             remote(own_block(h), kv.at[0, h], kv_send.at[2, h], kv_recv.at[0, h], group, sibling),
         )
 
-    first = pl.multiple_of(half * (group % 2), 128)
-    second = pl.multiple_of(half - half * (group % 2), 128)
-
-    def cut(start, index):
-        return pl.ds(pl.multiple_of(start + index * piece, 128), piece)
-
-    def send_piece(i):
+    mine = group % 4
+    quarters = (
+        mine,
+        mine + 1 - 2 * (mine % 2),
+        mine + 2 - 4 * (mine // 2),
+        3 - mine,
+    )
+
+    def cut(k):
+        return pl.ds(pl.multiple_of((2 * quarters[k // 2] + k % 2) * piece, 16), piece)
+
+    def send_piece(k):
         begin(
             None,
             remote(
-                weight_hbm.at[:, cut(first, i)],
-                weight.at[member, :, cut(first, i)],
-                w_send.at[i],
-                w_recv.at[i],
+                weight_hbm.at[cut(k)],
+                weight.at[member, cut(k)],
+                w_send.at[k],
+                w_recv.at[k],
                 group,
                 opposite,
             ),
@@ -224,25 +231,27 @@
     def send_sibling():
         begin(
             None,
-            remote(weight_hbm, weight.at[member], w_send.at[3], w_recv.at[6], group, sibling),
+            remote(weight_hbm, weight.at[member], w_send.at[2], w_recv.at[8], group, sibling),
         )
 
     def arrived(target, sem):
         remote(target, target, w_send.at[0], sem, group, sibling).wait_recv()
 
-    def take_piece(i):
-        start = first if i < 3 else second
-        block = weight.at[opposite, :, cut(start, i % 3)]
-        arrived(block, w_recv.at[i])
-        if i < 3:
-            begin(
-                None,
-                remote(block, block, w_pass.at[i], w_recv.at[3 + i], across, member),
-            )
-        begin(
-            None,
-            remote(block, block, w_pass.at[3 + i], w_recv.at[7 + i], group, sibling),
-        )
+    def take_piece(k):
+        block = weight.at[opposite, cut(k)]
+        arrived(block, w_recv.at[k])
+
+        def pass_on(sem, into, to_group, to_member):
+            begin(None, remote(block, block, w_pass.at[sem], w_recv.at[into], to_group, to_member))
+
+        if k < 2:
+            pass_on(8 + k, 2 + k, beside, member)
+            pass_on(10 + k, 4 + k, along, member)
+        if k == 3:
+            pass_on(12, 7, along, member)
+        if k == 4:
+            pass_on(13, 6, beside, member)
+        pass_on(k, 9 + k, group, sibling)
 
     scale = (HEAD ** -0.5) * math.log2(math.e)
 
@@ -314,28 +323,35 @@
     def finish_head(h):
         attended[:, h * HEAD : (h + 1) * HEAD] = jnp.transpose(acc[h] / total[h]).astype(jnp.bfloat16)
 
-    for i in range(3):
-        send_piece(i)
-        send_near(i)
-    for h in range(3, heads):
+    send_piece(0)
+    send_piece(1)
+    for h in range(heads):
         send_near(h)
     send_opposite(0)
+    send_opposite(1)
     send_sibling()
 
     load_qkv.wait()
     start_head(0)
+    receive(0, 0)
     start_head(1)
-    receive(0, 0)
     receive(0, 1)
     take_piece(0)
-    send_opposite(1)
-    for h in range(2, heads):
+    for h in range(2, heads - 1):
+        send_opposite(h)
+    start_head(2)
+    receive(0, 2)
+    take_piece(1)
+    send_opposite(heads - 1)
+    for h in range(3, heads):
         start_head(h)
         receive(0, h)
     attend_frame(0, 0)
+    take_piece(2)
+    take_piece(4)
     attend_frame(0, 1)
-    take_piece(1)
-    send_opposite(2)
+    take_piece(3)
+    take_piece(5)
     for h in range(2, heads):
         attend_frame(0, h)
     load_gates.wait()
@@ -343,14 +359,12 @@
     gate_row[...] = jnp.sum(
         jnp.where(step_index == steps_ref[member], gates[...], 0.0), axis=0, keepdims=True
     )
-    take_piece(2)
-    for h in range(3, heads):
-        send_opposite(h)
     for h in range(heads):
         receive(1, h)
         if h >= 1:
             receive(2, h - 1)
-            take_piece(2 + min(h, 3))
+        if h < 2:
+            take_piece(6 + h)
         attend_frame(1, h)
         if h >= 1:
             attend_frame(2, h - 1)
@@ -374,15 +388,15 @@
     load_latents.wait()
     project(member, 0, half)
     project(member, half, half)
-    arrived(weight.at[sibling], w_recv.at[6])
+    arrived(weight.at[sibling], w_recv.at[8])
     project(sibling, 0, half)
     project(sibling, half, half)
-    project(opposite, first, half)
-    project(opposite, second, half)
-    for i in range(6):
-        arrived(weight.at[far, :, cut(first if i < 3 else second, i % 3)], w_recv.at[7 + i])
-        if i % 3 == 2:
-            project(far, first if i < 3 else second, half)
+    project(opposite, 0, half)
+    project(opposite, half, half)
+    for k in range(8):
+        arrived(weight.at[far, cut(k)], w_recv.at[9 + k])
+    project(far, 0, half)
+    project(far, half, half)
 
     for condition, copy in sent:
         if condition is None:
@@ -417,9 +431,9 @@
             pltpu.SemaphoreType.DMA((3, heads)),
             pltpu.SemaphoreType.DMA((2, heads)),
             pltpu.SemaphoreType.DMA((3, heads)),
-            pltpu.SemaphoreType.DMA((4,)),
-            pltpu.SemaphoreType.DMA((9,)),
-            pltpu.SemaphoreType.DMA((13,)),
+            pltpu.SemaphoreType.DMA((3,)),
+            pltpu.SemaphoreType.DMA((14,)),
+            pltpu.SemaphoreType.DMA((17,)),
         ],
         compiler_params=pltpu.CompilerParams(
             collective_id=0, has_side_effects=True, vmem_limit_bytes=56 * 1024 * 1024
@@ -445,7 +459,7 @@
 
     def local(latents, projected, out_weight, gate_table, timesteps):
         one_frame_each = latents.shape[0] == FRAME_TOK and timesteps.shape[0] == members
-        if one_frame_each and members == 4 and groups % 2 == 0:
+        if one_frame_each and members == 4 and groups % 4 == 0:
             return frame_body(latents, projected, out_weight, gate_table, timesteps, groups)
         return body(latents, projected, out_weight, gate_table, timesteps)
 

time: 30.3 us -> 32.4 us (1.069)
  the two profiles are of different devices: /device:TPU:3 before, /device:TPU:21 now
where the time goes in v4:
time: 32.4 us; the launch traced here: 32.2 us
  Pallas kernels  31.1 us (96%)
  local copies, waits for them, and re-layouts  1.15 us (4%)
    pallas_call x1, Pallas kernels, frame_body(): pl.pallas_call(functools.partial(frame_kernel, groups), out_shape=pltpu.V...  31.1 us
    unnamed x1, local copies, waits for them, and re-layouts  1.15 us

profile of v4, /device:TPU:21, one launch (start us, length us, event | category | flops | bytes accessed | tf_op | source)
XLA Modules:
  0.0 32.2 jit_solution(7978626567088323990)
XLA Ops:
  0.0 31.1 %shard_map.55 = bf16[256,3072]{1,0:T(8,128)(2,1)S(1)} custom-call(s32[4]{0:T(128)} %steps_ref.1, bf16[256,3072]{1,0:T(8,128)(2,1)} %latents_hbm.1, bf16[3,256,512]{2,1,0:T(8,128)(2,1)} %bitcast.1, bf16[512,768]{1,0:T(8,128)(2,1)} %weight_hbm.1, f32[40,3072]{1,0:T(8,128)} %gates_hbm.1), custom_call_target="tpu_custom_call" | custom-call | flops 1342177280 | bytes 6291456 | tf_op jit(solution)/shard_map/pallas_call | solution.py:414
  31.1 1.1 %copy.7 = bf16[256,3072]{1,0:T(8,128)(2,1)} copy(bf16[256,3072]{1,0:T(8,128)(2,1)S(1)} %shard_map.55) | data formatting | bytes 3145728

commit v5 on v4

--- a/solution.py
+++ b/solution.py
@@ -163,11 +163,17 @@
     def _():
         greet(group - 1, member + 1)
 
-    load_qkv = pltpu.make_async_copy(qkv_hbm, qkv, local_sem.at[0])
-    load_weight = pltpu.make_async_copy(weight_hbm, weight.at[member], local_sem.at[1])
-    load_latents = pltpu.make_async_copy(latents_hbm, latents, local_sem.at[2])
-    load_gates = pltpu.make_async_copy(gates_hbm, gates, local_sem.at[3])
-    load_qkv.start()
+    load_heads = [
+        pltpu.make_async_copy(
+            qkv_hbm.at[:, :, pl.ds(h * HEAD, HEAD)], qkv.at[h], local_sem.at[3 + h]
+        )
+        for h in range(heads)
+    ]
+    load_weight = pltpu.make_async_copy(weight_hbm, weight.at[member], local_sem.at[0])
+    load_latents = pltpu.make_async_copy(latents_hbm, latents, local_sem.at[1])
+    load_gates = pltpu.make_async_copy(gates_hbm, gates, local_sem.at[2])
+    for load in load_heads:
+        load.start()
     load_weight.start()
     load_gates.start()
     load_latents.start()
@@ -184,7 +190,7 @@
             pl.when(condition)(copy.start)
 
     def own_block(h):
-        return qkv_hbm.at[pl.ds(1, 2), :, pl.ds(h * HEAD, HEAD)]
+        return qkv.at[h, pl.ds(1, 2)]
 
     def send_opposite(h):
         begin(
@@ -256,7 +262,7 @@
     scale = (HEAD ** -0.5) * math.log2(math.e)
 
     def own_head(index, h):
-        return qkv[index, :, h * HEAD : (h + 1) * HEAD]
+        return qkv[h, index]
 
     def scores_of(h, keys):
         return (
@@ -323,26 +329,22 @@
     def finish_head(h):
         attended[:, h * HEAD : (h + 1) * HEAD] = jnp.transpose(acc[h] / total[h]).astype(jnp.bfloat16)
 
-    send_piece(0)
-    send_piece(1)
     for h in range(heads):
+        load_heads[h].wait()
+        send_opposite(h)
+        if h < 2:
+            send_piece(h)
         send_near(h)
-    send_opposite(0)
-    send_opposite(1)
     send_sibling()
 
-    load_qkv.wait()
     start_head(0)
     receive(0, 0)
     start_head(1)
     receive(0, 1)
     take_piece(0)
-    for h in range(2, heads - 1):
-        send_opposite(h)
     start_head(2)
     receive(0, 2)
     take_piece(1)
-    send_opposite(heads - 1)
     for h in range(3, heads):
         start_head(h)
         receive(0, h)
@@ -417,7 +419,7 @@
         in_specs=[pl.BlockSpec(memory_space=pltpu.SMEM)] + [in_hbm] * 4,
         out_specs=pl.BlockSpec(memory_space=pltpu.VMEM),
         scratch_shapes=[
-            pltpu.VMEM((3, rows, inner), jnp.bfloat16),
+            pltpu.VMEM((heads, 3, rows, HEAD), jnp.bfloat16),
             pltpu.VMEM((3, heads, 2, rows, HEAD), jnp.bfloat16),
             pltpu.VMEM((4, inner, columns), jnp.bfloat16),
             pltpu.VMEM((rows, width), jnp.bfloat16),
@@ -427,7 +429,7 @@
             pltpu.VMEM((heads, 1, rows), jnp.float32),
             pltpu.VMEM((heads, HEAD, rows), jnp.float32),
             pltpu.VMEM((rows, inner), jnp.bfloat16),
-            pltpu.SemaphoreType.DMA((4,)),
+            pltpu.SemaphoreType.DMA((3 + heads,)),
             pltpu.SemaphoreType.DMA((3, heads)),
             pltpu.SemaphoreType.DMA((2, heads)),
             pltpu.SemaphoreType.DMA((3, heads)),

time: 32.4 us -> 32.2 us (level)
  no operation moved by 1% of the time
where the time goes in v5:
time: 32.2 us; the launch traced here: 32.1 us
  Pallas kernels  30.9 us (96%)
  local copies, waits for them, and re-layouts  1.15 us (4%)
    pallas_call x1, Pallas kernels, frame_body(): pl.pallas_call(functools.partial(frame_kernel, groups), out_shape=pltpu.V...  30.9 us
    unnamed x1, local copies, waits for them, and re-layouts  1.15 us

profile of v5, /device:TPU:21, one launch (start us, length us, event | category | flops | bytes accessed | tf_op | source)
XLA Modules:
  0.0 32.1 jit_solution(6495213482077502290)
XLA Ops:
  0.0 30.9 %shard_map.55 = bf16[256,3072]{1,0:T(8,128)(2,1)S(1)} custom-call(s32[4]{0:T(128)} %steps_ref.1, bf16[256,3072]{1,0:T(8,128)(2,1)} %latents_hbm.1, bf16[3,256,512]{2,1,0:T(8,128)(2,1)} %bitcast.1, bf16[512,768]{1,0:T(8,128)(2,1)} %weight_hbm.1, f32[40,3072]{1,0:T(8,128)} %gates_hbm.1), custom_call_target="tpu_custom_call" | custom-call | flops 1342177280 | bytes 6291456 | tf_op jit(solution)/shard_map/pallas_call | solution.py:416
  30.9 1.1 %copy.7 = bf16[256,3072]{1,0:T(8,128)(2,1)} copy(bf16[256,3072]{1,0:T(8,128)(2,1)S(1)} %shard_map.55) | data formatting | bytes 3145728

commit v6 on v5

--- a/solution.py
+++ b/solution.py
@@ -103,6 +103,7 @@
     out,
     qkv,
     kv,
+    relay,
     weight,
     latents,
     gates,
@@ -118,6 +119,9 @@
     w_send,
     w_pass,
     w_recv,
+    relay_send,
+    relay_pass,
+    relay_recv,
 ):
     heads = kv.shape[1]
     columns = weight.shape[2]
@@ -133,6 +137,10 @@
     has_next = jnp.logical_and(member >= 1, group < groups - 1)
     has_previous = jnp.logical_and(member <= 2, group >= 1)
 
+    by_way = heads // 2
+    relays = jnp.logical_and(member == 0, group < groups - 1)
+    has_relay = jnp.logical_and(member == 1, group >= 1)
+
     def remote(source, target, send_sem, recv_sem, to_group, to_member):
         return pltpu.make_async_remote_copy(
             src_ref=source,
@@ -162,6 +170,14 @@
     @pl.when(has_previous)
     def _():
         greet(group - 1, member + 1)
+
+    @pl.when(relays)
+    def _():
+        greet(group + 1, 1)
+
+    @pl.when(has_relay)
+    def _():
+        greet(group - 1, 0)
 
     load_heads = [
         pltpu.make_async_copy(
@@ -178,7 +194,10 @@
     load_gates.start()
     load_latents.start()
 
-    pl.semaphore_wait(barrier, 4 + has_next.astype(jnp.int32) + has_previous.astype(jnp.int32))
+    peers = 4
+    for present in (has_next, has_previous, relays, has_relay):
+        peers = peers + present.astype(jnp.int32)
+    pl.semaphore_wait(barrier, peers)
 
     sent = []
 
@@ -199,8 +218,17 @@
         )
 
     def send_near(h):
+        direct = has_next
+        if h < by_way:
+            direct = jnp.logical_and(has_next, member != 2)
+            begin(
+                jnp.logical_and(has_next, member == 2),
+                remote(
+                    own_block(h), relay.at[h], relay_send.at[h], relay_recv.at[h], group, opposite
+                ),
+            )
         begin(
-            has_next,
+            direct,
             remote(
                 own_block(h), kv.at[2, h], kv_send.at[1, h], kv_recv.at[2, h], group + 1, member - 1
             ),
@@ -208,6 +236,14 @@
         begin(
             core == 0,
             remote(own_block(h), kv.at[0, h], kv_send.at[2, h], kv_recv.at[0, h], group, sibling),
+        )
+
+    def pass_relay(h):
+        block = relay.at[h]
+        pl.when(relays)(lambda: arrived(block, relay_recv.at[h]))
+        begin(
+            relays,
+            remote(block, kv.at[2, h], relay_pass.at[h], kv_recv.at[2, h], group + 1, member + 1),
         )
 
     mine = group % 4
@@ -329,31 +365,40 @@
     def finish_head(h):
         attended[:, h * HEAD : (h + 1) * HEAD] = jnp.transpose(acc[h] / total[h]).astype(jnp.bfloat16)
 
+    send_piece(0)
+    send_piece(1)
     for h in range(heads):
         load_heads[h].wait()
+        send_near(h)
+    send_opposite(0)
+    send_sibling()
+
+    start_head(0)
+    start_head(1)
+    receive(0, 0)
+    take_piece(0)
+    for h in range(1, heads - 1):
         send_opposite(h)
-        if h < 2:
-            send_piece(h)
-        send_near(h)
-    send_sibling()
-
-    start_head(0)
-    receive(0, 0)
-    start_head(1)
+    start_head(2)
     receive(0, 1)
-    take_piece(0)
-    start_head(2)
-    receive(0, 2)
     take_piece(1)
+    send_opposite(heads - 1)
     for h in range(3, heads):
         start_head(h)
+    for h in range(by_way):
+        pass_relay(h)
+    take_piece(2)
+    take_piece(4)
+    for h in range(2, heads):
         receive(0, h)
     attend_frame(0, 0)
-    take_piece(2)
-    take_piece(4)
-    attend_frame(0, 1)
     take_piece(3)
     take_piece(5)
+    receive(1, 0)
+    attend_frame(0, 1)
+    take_piece(6)
+    take_piece(7)
+    receive(1, 1)
     for h in range(2, heads):
         attend_frame(0, h)
     load_gates.wait()
@@ -362,11 +407,10 @@
         jnp.where(step_index == steps_ref[member], gates[...], 0.0), axis=0, keepdims=True
     )
     for h in range(heads):
-        receive(1, h)
+        if h >= 2:
+            receive(1, h)
         if h >= 1:
             receive(2, h - 1)
-        if h < 2:
-            take_piece(6 + h)
         attend_frame(1, h)
         if h >= 1:
             attend_frame(2, h - 1)
@@ -421,6 +465,7 @@
         scratch_shapes=[
             pltpu.VMEM((heads, 3, rows, HEAD), jnp.bfloat16),
             pltpu.VMEM((3, heads, 2, rows, HEAD), jnp.bfloat16),
+            pltpu.VMEM((heads // 2, 2, rows, HEAD), jnp.bfloat16),
             pltpu.VMEM((4, inner, columns), jnp.bfloat16),
             pltpu.VMEM((rows, width), jnp.bfloat16),
             pltpu.VMEM(gate_table.shape, jnp.float32),
@@ -436,6 +481,9 @@
             pltpu.SemaphoreType.DMA((3,)),
             pltpu.SemaphoreType.DMA((14,)),
             pltpu.SemaphoreType.DMA((17,)),
+            pltpu.SemaphoreType.DMA((heads // 2,)),
+            pltpu.SemaphoreType.DMA((heads // 2,)),
+            pltpu.SemaphoreType.DMA((heads // 2,)),
         ],
         compiler_params=pltpu.CompilerParams(
             collective_id=0, has_side_effects=True, vmem_limit_bytes=56 * 1024 * 1024

time: 32.2 us -> 31.8 us (0.988)
  the two profiles are of different devices: /device:TPU:21 before, /device:TPU:25 now
where the time goes in v6:
time: 31.8 us; the launch traced here: 31.7 us
  Pallas kernels  30.5 us (96%)
  local copies, waits for them, and re-layouts  1.15 us (4%)
    pallas_call x1, Pallas kernels, frame_body(): pl.pallas_call(functools.partial(frame_kernel, groups), out_shape=pltpu.V...  30.5 us
    unnamed x1, local copies, waits for them, and re-layouts  1.15 us

profile of v6, /device:TPU:25, one launch (start us, length us, event | category | flops | bytes accessed | tf_op | source)
XLA Modules:
  0.0 31.7 jit_solution(9850363593874215417)
XLA Ops:
  0.0 30.5 %shard_map.55 = bf16[256,3072]{1,0:T(8,128)(2,1)S(1)} custom-call(s32[4]{0:T(128)} %steps_ref.1, bf16[256,3072]{1,0:T(8,128)(2,1)} %latents_hbm.1, bf16[3,256,512]{2,1,0:T(8,128)(2,1)} %bitcast.1, bf16[512,768]{1,0:T(8,128)(2,1)} %weight_hbm.1, f32[40,3072]{1,0:T(8,128)} %gates_hbm.1), custom_call_target="tpu_custom_call" | custom-call | flops 1342177280 | bytes 6291456 | tf_op jit(solution)/shard_map/pallas_call | solution.py:460
  30.5 1.1 %copy.7 = bf16[256,3072]{1,0:T(8,128)(2,1)} copy(bf16[256,3072]{1,0:T(8,128)(2,1)S(1)} %shard_map.55) | data formatting | bytes 3145728

commit v7 on v6

--- a/solution.py
+++ b/solution.py
@@ -112,6 +112,7 @@
     total,
     acc,
     attended,
+    partial,
     local_sem,
     kv_send,
     kv_pass,
@@ -137,7 +138,7 @@
     has_next = jnp.logical_and(member >= 1, group < groups - 1)
     has_previous = jnp.logical_and(member <= 2, group >= 1)
 
-    by_way = heads // 2
+    by_way = 1
     relays = jnp.logical_and(member == 0, group < groups - 1)
     has_relay = jnp.logical_and(member == 1, group >= 1)
 
@@ -415,34 +416,46 @@
         if h >= 1:
             attend_frame(2, h - 1)
             finish_head(h - 1)
+    done = (heads - 1) * HEAD
+    early = (member, sibling, opposite)
+    load_weight.wait()
+    load_latents.wait()
+    arrived(weight.at[sibling], w_recv.at[8])
+    for i, owner in enumerate(early):
+        for start in (0, half):
+            partial[i, :, start : start + half] = jnp.dot(
+                attended[:, :done],
+                weight[owner, :done, start : start + half],
+                preferred_element_type=jnp.float32,
+            )
+
     receive(2, heads - 1)
     attend_frame(2, heads - 1)
     finish_head(heads - 1)
 
-    def project(owner, start, width):
-        place = pl.ds(pl.multiple_of(owner * columns + start, 128), width)
-        branch = jnp.dot(
-            attended[...],
-            weight[owner, :, pl.ds(start, width)],
-            preferred_element_type=jnp.float32,
-        )
+    def update(owner, start, branch):
+        place = pl.ds(pl.multiple_of(owner * columns + start, 128), half)
         out[:, place] = (
             latents[:, place].astype(jnp.float32) + gate_row[:, place] * branch
         ).astype(jnp.bfloat16)
 
-    load_weight.wait()
-    load_latents.wait()
-    project(member, 0, half)
-    project(member, half, half)
-    arrived(weight.at[sibling], w_recv.at[8])
-    project(sibling, 0, half)
-    project(sibling, half, half)
-    project(opposite, 0, half)
-    project(opposite, half, half)
+    for i, owner in enumerate(early):
+        for start in (0, half):
+            branch = partial[i, :, start : start + half] + jnp.dot(
+                attended[:, done:],
+                weight[owner, done:, start : start + half],
+                preferred_element_type=jnp.float32,
+            )
+            update(owner, start, branch)
     for k in range(8):
         arrived(weight.at[far, cut(k)], w_recv.at[9 + k])
-    project(far, 0, half)
-    project(far, half, half)
+    for start in (0, half):
+        branch = jnp.dot(
+            attended[...],
+            weight[far, :, start : start + half],
+            preferred_element_type=jnp.float32,
+        )
+        update(far, start, branch)
 
     for condition, copy in sent:
         if condition is None:
@@ -465,7 +478,7 @@
         scratch_shapes=[
             pltpu.VMEM((heads, 3, rows, HEAD), jnp.bfloat16),
             pltpu.VMEM((3, heads, 2, rows, HEAD), jnp.bfloat16),
-            pltpu.VMEM((heads // 2, 2, rows, HEAD), jnp.bfloat16),
+            pltpu.VMEM((1, 2, rows, HEAD), jnp.bfloat16),
             pltpu.VMEM((4, inner, columns), jnp.bfloat16),
             pltpu.VMEM((rows, width), jnp.bfloat16),
             pltpu.VMEM(gate_table.shape, jnp.float32),
@@ -474,6 +487,7 @@
             pltpu.VMEM((heads, 1, rows), jnp.float32),
             pltpu.VMEM((heads, HEAD, rows), jnp.float32),
             pltpu.VMEM((rows, inner), jnp.bfloat16),
+            pltpu.VMEM((3, rows, columns), jnp.float32),
             pltpu.SemaphoreType.DMA((3 + heads,)),
             pltpu.SemaphoreType.DMA((3, heads)),
             pltpu.SemaphoreType.DMA((2, heads)),
@@ -481,9 +495,9 @@
             pltpu.SemaphoreType.DMA((3,)),
             pltpu.SemaphoreType.DMA((14,)),
             pltpu.SemaphoreType.DMA((17,)),
-            pltpu.SemaphoreType.DMA((heads // 2,)),
-            pltpu.SemaphoreType.DMA((heads // 2,)),
-            pltpu.SemaphoreType.DMA((heads // 2,)),
+            pltpu.SemaphoreType.DMA((1,)),
+            pltpu.SemaphoreType.DMA((1,)),
+            pltpu.SemaphoreType.DMA((1,)),
         ],
         compiler_params=pltpu.CompilerParams(
             collective_id=0, has_side_effects=True, vmem_limit_bytes=56 * 1024 * 1024

time: 31.8 us -> 32.3 us (1.016)
  the two profiles are of different devices: /device:TPU:25 before, /device:TPU:21 now
where the time goes in v7:
time: 32.3 us; the launch traced here: 32.1 us
  Pallas kernels  30.9 us (96%)
  local copies, waits for them, and re-layouts  1.15 us (4%)
    pallas_call x1, Pallas kernels, frame_body(): pl.pallas_call(functools.partial(frame_kernel, groups), out_shape=pltpu.V...  30.9 us
    unnamed x1, local copies, waits for them, and re-layouts  1.15 us

profile of v7, /device:TPU:21, one launch (start us, length us, event | category | flops | bytes accessed | tf_op | source)
XLA Modules:
  0.0 32.1 jit_solution(10141851759266121811)
XLA Ops:
  0.0 30.9 %shard_map.55 = bf16[256,3072]{1,0:T(8,128)(2,1)S(1)} custom-call(s32[4]{0:T(128)} %steps_ref.1, bf16[256,3072]{1,0:T(8,128)(2,1)} %latents_hbm.1, bf16[3,256,512]{2,1,0:T(8,128)(2,1)} %bitcast.1, bf16[512,768]{1,0:T(8,128)(2,1)} %weight_hbm.1, f32[40,3072]{1,0:T(8,128)} %gates_hbm.1), custom_call_target="tpu_custom_call" | custom-call | flops 1342177280 | bytes 6291456 | tf_op jit(solution)/shard_map/pallas_call | solution.py:473
  31.0 1.1 %copy.7 = bf16[256,3072]{1,0:T(8,128)(2,1)} copy(bf16[256,3072]{1,0:T(8,128)(2,1)S(1)} %shard_map.55) | data formatting | bytes 3145728

commit v8 on v5

--- a/solution.py
+++ b/solution.py
@@ -125,8 +125,7 @@
     piece = weight.shape[1] // 8
     group, member = lax.axis_index("tm"), lax.axis_index("fsdp")
     row, core = member // 2, member % 2
-    beside = group + 1 - 2 * (group % 2)
-    along = group + 2 - 4 * ((group // 2) % 2)
+    across = group + 1 - 2 * (group % 2)
     sibling = member + 1 - 2 * core
     opposite = member + 2 - 4 * row
     far = 3 - member
@@ -152,8 +151,7 @@
 
     greet(group, sibling)
     greet(group, opposite)
-    greet(beside, member)
-    greet(along, member)
+    greet(across, member)
 
     @pl.when(has_next)
     def _():
@@ -178,7 +176,7 @@
     load_gates.start()
     load_latents.start()
 
-    pl.semaphore_wait(barrier, 4 + has_next.astype(jnp.int32) + has_previous.astype(jnp.int32))
+    pl.semaphore_wait(barrier, 3 + has_next.astype(jnp.int32) + has_previous.astype(jnp.int32))
 
     sent = []
 
@@ -210,16 +208,9 @@
             remote(own_block(h), kv.at[0, h], kv_send.at[2, h], kv_recv.at[0, h], group, sibling),
         )
 
-    mine = group % 4
-    quarters = (
-        mine,
-        mine + 1 - 2 * (mine % 2),
-        mine + 2 - 4 * (mine // 2),
-        3 - mine,
-    )
-
     def cut(k):
-        return pl.ds(pl.multiple_of((2 * quarters[k // 2] + k % 2) * piece, 16), piece)
+        part = group % 2 if k < 4 else 1 - group % 2
+        return pl.ds(pl.multiple_of((4 * part + k % 4) * piece, 16), piece)
 
     def send_piece(k):
         begin(
@@ -237,7 +228,7 @@
     def send_sibling():
         begin(
             None,
-            remote(weight_hbm, weight.at[member], w_send.at[2], w_recv.at[8], group, sibling),
+            remote(weight_hbm, weight.at[member], w_send.at[4], w_recv.at[8], group, sibling),
         )
 
     def arrived(target, sem):
@@ -246,18 +237,15 @@
     def take_piece(k):
         block = weight.at[opposite, cut(k)]
         arrived(block, w_recv.at[k])
-
-        def pass_on(sem, into, to_group, to_member):
-            begin(None, remote(block, block, w_pass.at[sem], w_recv.at[into], to_group, to_member))
-
-        if k < 2:
-            pass_on(8 + k, 2 + k, beside, member)
-            pass_on(10 + k, 4 + k, along, member)
-        if k == 3:
-            pass_on(12, 7, along, member)
-        if k == 4:
-            pass_on(13, 6, beside, member)
-        pass_on(k, 9 + k, group, sibling)
+        if k < 4:
+            begin(
+                None,
+                remote(block, block, w_pass.at[8 + k], w_recv.at[4 + k], across, member),
+            )
+        begin(
+            None,
+            remote(block, block, w_pass.at[k], w_recv.at[9 + k], group, sibling),
+        )
 
     scale = (HEAD ** -0.5) * math.log2(math.e)
 
@@ -329,32 +317,33 @@
     def finish_head(h):
         attended[:, h * HEAD : (h + 1) * HEAD] = jnp.transpose(acc[h] / total[h]).astype(jnp.bfloat16)
 
+    for k in range(4):
+        send_piece(k)
     for h in range(heads):
         load_heads[h].wait()
-        send_opposite(h)
-        if h < 2:
-            send_piece(h)
         send_near(h)
+    send_opposite(0)
     send_sibling()
 
     start_head(0)
+    start_head(1)
     receive(0, 0)
-    start_head(1)
+    take_piece(0)
     receive(0, 1)
-    take_piece(0)
-    start_head(2)
-    receive(0, 2)
-    take_piece(1)
-    for h in range(3, heads):
+    send_opposite(1)
+    for h in range(2, heads):
         start_head(h)
         receive(0, h)
     attend_frame(0, 0)
+    take_piece(1)
+    send_opposite(2)
+    attend_frame(0, 1)
     take_piece(2)
-    take_piece(4)
-    attend_frame(0, 1)
+    for h in range(3, heads):
+        send_opposite(h)
+    attend_frame(0, 2)
     take_piece(3)
-    take_piece(5)
-    for h in range(2, heads):
+    for h in range(3, heads):
         attend_frame(0, h)
     load_gates.wait()
     step_index = lax.broadcasted_iota(jnp.int32, gates.shape, 0)
@@ -363,10 +352,10 @@
     )
     for h in range(heads):
         receive(1, h)
+        if h < 4:
+            take_piece(4 + h)
         if h >= 1:
             receive(2, h - 1)
-        if h < 2:
-            take_piece(6 + h)
         attend_frame(1, h)
         if h >= 1:
             attend_frame(2, h - 1)
@@ -433,8 +422,8 @@
             pltpu.SemaphoreType.DMA((3, heads)),
             pltpu.SemaphoreType.DMA((2, heads)),
             pltpu.SemaphoreType.DMA((3, heads)),
-            pltpu.SemaphoreType.DMA((3,)),
-            pltpu.SemaphoreType.DMA((14,)),
+            pltpu.SemaphoreType.DMA((5,)),
+            pltpu.SemaphoreType.DMA((12,)),
             pltpu.SemaphoreType.DMA((17,)),
         ],
         compiler_params=pltpu.CompilerParams(
@@ -461,7 +450,7 @@
 
     def local(latents, projected, out_weight, gate_table, timesteps):
         one_frame_each = latents.shape[0] == FRAME_TOK and timesteps.shape[0] == members
-        if one_frame_each and members == 4 and groups % 4 == 0:
+        if one_frame_each and members == 4 and groups % 2 == 0:
             return frame_body(latents, projected, out_weight, gate_table, timesteps, groups)
         return body(latents, projected, out_weight, gate_table, timesteps)
 

time: 32.2 us -> 30.3 us (0.941)
  the two profiles are of different devices: /device:TPU:21 before, /device:TPU:9 now
where the time goes in v8:
time: 30.3 us; the launch traced here: 30.1 us
  Pallas kernels  29 us (96%)
  local copies, waits for them, and re-layouts  1.15 us (4%)
    pallas_call x1, Pallas kernels, frame_body(): pl.pallas_call(functools.partial(frame_kernel, groups), out_shape=pltpu.V...  29 us
    unnamed x1, local copies, waits for them, and re-layouts  1.15 us

profile of v8, /device:TPU:9, one launch (start us, length us, event | category | flops | bytes accessed | tf_op | source)
XLA Modules:
  0.0 30.1 jit_solution(3663681027149958069)
XLA Ops:
  0.0 29.0 %shard_map.55 = bf16[256,3072]{1,0:T(8,128)(2,1)S(1)} custom-call(s32[4]{0:T(128)} %steps_ref.1, bf16[256,3072]{1,0:T(8,128)(2,1)} %latents_hbm.1, bf16[3,256,512]{2,1,0:T(8,128)(2,1)} %bitcast.1, bf16[512,768]{1,0:T(8,128)(2,1)} %weight_hbm.1, f32[40,3072]{1,0:T(8,128)} %gates_hbm.1), custom_call_target="tpu_custom_call" | custom-call | flops 1342177280 | bytes 6291456 | tf_op jit(solution)/shard_map/pallas_call | solution.py:405
  29.0 1.1 %copy.7 = bf16[256,3072]{1,0:T(8,128)(2,1)} copy(bf16[256,3072]{1,0:T(8,128)(2,1)S(1)} %shard_map.55) | data formatting | bytes 3145728

commit v9 on v8

--- a/solution.py
+++ b/solution.py
@@ -323,6 +323,7 @@
         load_heads[h].wait()
         send_near(h)
     send_opposite(0)
+    send_opposite(1)
     send_sibling()
 
     start_head(0)
@@ -330,17 +331,16 @@
     receive(0, 0)
     take_piece(0)
     receive(0, 1)
-    send_opposite(1)
+    send_opposite(2)
     for h in range(2, heads):
         start_head(h)
         receive(0, h)
     attend_frame(0, 0)
     take_piece(1)
-    send_opposite(2)
+    for h in range(3, heads):
+        send_opposite(h)
     attend_frame(0, 1)
     take_piece(2)
-    for h in range(3, heads):
-        send_opposite(h)
     attend_frame(0, 2)
     take_piece(3)
     for h in range(3, heads):
@@ -351,9 +351,9 @@
         jnp.where(step_index == steps_ref[member], gates[...], 0.0), axis=0, keepdims=True
     )
     for h in range(heads):
-        receive(1, h)
         if h < 4:
             take_piece(4 + h)
+        receive(1, h)
         if h >= 1:
             receive(2, h - 1)
         attend_frame(1, h)

time: 30.3 us -> 30.3 us (level)
  the two profiles are of different devices: /device:TPU:9 before, /device:TPU:21 now
where the time goes in v9:
time: 30.3 us; the launch traced here: 29.9 us
  Pallas kernels  28.7 us (95%)
  local copies, waits for them, and re-layouts  1.15 us (4%)
    pallas_call x1, Pallas kernels, frame_body(): pl.pallas_call(functools.partial(frame_kernel, groups), out_shape=pltpu.V...  28.7 us
    unnamed x1, local copies, waits for them, and re-layouts  1.15 us

profile of v9, /device:TPU:21, one launch (start us, length us, event | category | flops | bytes accessed | tf_op | source)
XLA Modules:
  0.0 29.9 jit_solution(15188141974257694604)
XLA Ops:
  0.0 28.7 %shard_map.55 = bf16[256,3072]{1,0:T(8,128)(2,1)S(1)} custom-call(s32[4]{0:T(128)} %steps_ref.1, bf16[256,3072]{1,0:T(8,128)(2,1)} %latents_hbm.1, bf16[3,256,512]{2,1,0:T(8,128)(2,1)} %bitcast.1, bf16[512,768]{1,0:T(8,128)(2,1)} %weight_hbm.1, f32[40,3072]{1,0:T(8,128)} %gates_hbm.1), custom_call_target="tpu_custom_call" | custom-call | flops 1342177280 | bytes 6291456 | tf_op jit(solution)/shard_map/pallas_call | solution.py:405
  28.7 1.1 %copy.7 = bf16[256,3072]{1,0:T(8,128)(2,1)} copy(bf16[256,3072]{1,0:T(8,128)(2,1)S(1)} %shard_map.55) | data formatting | bytes 3145728
